TPU v7x, 512 devices: a whole 4x4x16 slice. The times are simulated.
512 devices in a mesh: head: 8 (over y, core), ctx: 64 (over z, x).
Axes of the slice: x: 4, y: 4, z: 16, core: 2. Of those that a mesh axis runs over, the one named last changes fastest.
Arguments:
- main_query: bfloat16 [128, 128, 576], P(None, 'head'), may hold values from -36 to 36
- latent_keys: bfloat16 [65536, 576], P('ctx'), may hold values from -6 to 6
- index_query: bfloat16 [128, 64, 128], P('head'), may hold values from -0.96 to 0.96
- index_weight: bfloat16 [128, 64], P('head'), may hold values from -7.5 to 7.5
- index_keys: bfloat16 [65536, 128], P('ctx'), may hold values from -1.25 to 1.25
- query_positions: int32 [128], replicated, may hold values from 0 to 65535, as said below
Outputs:
- grad_index_query: float32 [128, 64, 128], P('head')
- grad_index_weight: float32 [128, 64], P('head')
- grad_index_keys: float32 [65536, 128], P('ctx')
Inputs may be any that keep to these rules, and one draw needn't show every extreme that they name: `query_positions`: strictly increasing over the rows; the last row sits at position 65535.
All inputs are finite; a program needn't handle non-finite values.
Results may differ from a plain program's by a relative error of at most 0.0042.
Values sent between devices are 32-bit elements; how exact they have to be, the bound alone decides.
A program may use at most 128 MiB of HBM per device.

v0:
```python
import jax
import jax.numpy as jnp
from jax import lax
from jax.sharding import PartitionSpec as P

main_scale = 192.0 ** (-0.5)
loss_scale = 256.0
masked_value = -1e30


def shards(main_query, latent_keys, index_query, index_weight, index_keys, query_positions):
    row_count, heads_dev, latent_dim = main_query.shape
    key_count = latent_keys.shape[0]
    total_heads = heads_dev * lax.axis_size("head")
    slab_start = lax.axis_index("ctx") * key_count
    key_positions = slab_start + lax.iota(jnp.int32, key_count)
    visible = key_positions[None, :] <= query_positions[:, None]
    flat_query = main_query.reshape(row_count * heads_dev, latent_dim)
    scores = (
        jnp.einsum("nd,sd->ns", flat_query, latent_keys, preferred_element_type=jnp.float32)
        * main_scale
    )
    scores = scores.reshape(row_count, heads_dev, key_count)
    masked = jnp.where(visible[:, None, :], scores, masked_value)
    own_rows, index_heads, index_dim = index_query.shape
    row_start = lax.axis_index("head") * own_rows
    own_positions = lax.dynamic_slice_in_dim(query_positions, row_start, own_rows, 0)
    own_visible = key_positions[None, :] <= own_positions[:, None]
    flat_index_query = index_query.reshape(own_rows * index_heads, index_dim)
    affinity = jnp.einsum(
        "nd,sd->ns", flat_index_query, index_keys, preferred_element_type=jnp.float32
    )
    affinity = affinity.reshape(own_rows, index_heads, key_count)
    weight = index_weight.astype(jnp.float32)
    logits = jnp.sum(weight[:, :, None] * jnp.maximum(affinity, 0.0), axis=1)
    index_masked = jnp.where(own_visible, logits, masked_value)
    main_max = jnp.max(masked, axis=2)
    index_max = jnp.max(index_masked, axis=1)
    main_max, index_max = lax.pmax((main_max, index_max), "ctx")
    main_total = jnp.sum(
        jnp.where(visible[:, None, :], jnp.exp(masked - main_max[:, :, None]), 0.0), axis=2
    )
    index_total = jnp.sum(
        jnp.where(own_visible, jnp.exp(index_masked - index_max[:, None]), 0.0), axis=1
    )
    main_total, index_total = lax.psum((main_total, index_total), "ctx")
    probs = (
        jnp.where(visible[:, None, :], jnp.exp(masked - main_max[:, :, None]), 0.0)
        / main_total[:, :, None]
    )
    whole = lax.psum(jnp.sum(probs, axis=1) / total_heads, "head")
    target = lax.dynamic_slice_in_dim(whole, row_start, own_rows, 0)
    index_probs = (
        jnp.where(own_visible, jnp.exp(index_masked - index_max[:, None]), 0.0)
        / index_total[:, None]
    )
    grad_logits = loss_scale * (index_probs - target)
    upstream = jnp.where(affinity > 0, grad_logits[:, None, :] * weight[:, :, None], 0.0).astype(
        jnp.bfloat16
    )
    flat_upstream = upstream.reshape(own_rows * index_heads, key_count)
    query_part = jnp.dot(flat_upstream, index_keys, preferred_element_type=jnp.float32).reshape(
        own_rows, index_heads, index_dim
    )
    weight_part = jnp.sum(grad_logits[:, None, :] * jnp.maximum(affinity, 0.0), axis=2)
    key_part = jnp.einsum(
        "ns,nd->sd", flat_upstream, flat_index_query, preferred_element_type=jnp.float32
    )
    grad_query, grad_weight = lax.psum((query_part, weight_part), "ctx")
    grad_keys = lax.psum(key_part, "head")
    return (grad_query, grad_weight, grad_keys)


def solution(mesh):
    in_specs = (
        P(None, "head", None),
        P("ctx", None),
        P("head", None, None),
        P("head", None),
        P("ctx", None),
        P(),
    )
    out_specs = (P("head", None, None), P("head", None), P("ctx", None))
    return jax.shard_map(shards, mesh=mesh, in_specs=in_specs, out_specs=out_specs, check_vma=False)
```

profile of v0, /device:TPU:1, one launch (start us, length us, event | category | flops | bytes accessed | tf_op | source)
XLA Modules:
  0.0 1012.9 jit_solution(17329749024597939206)
XLA Ops:
  7.2 0.0 copy-start
  7.2 0.0 copy-start.4
  7.2 0.0 all-reduce.6.cloned.1.call-start
  7.3 5.1 copy.9
  12.3 0.0 copy-done.4
  12.3 0.1 broadcast_compare_fusion
  12.5 0.0 copy-done
  12.5 0.0 copy-start.3
  12.5 0.0 copy-start.1
  12.5 0.0 copy-start.2
  12.5 8.2 fusion.2
  20.7 0.1 reduce_max.22
  20.8 0.0 copy-done.3
  20.8 0.1 dynamic_slice.6
  20.9 0.0 copy-done.1
  20.9 0.0 copy-done.2
  20.9 2.7 multiply_reduce_fusion.1
  23.6 0.2 fusion.20
  23.8 231.3 %all-reduce.1 = (f32[128,16]{1,0:T(8,128)S(1)}, f32[16]{0:T(128)S(1)}) all-reduce(f32[128,16]{1,0:T(8,128)S(1)} %reduce_max.22, f32[16]{0:T(128)S(1)} %fusion.20), channel_id=1, replica_groups=mesh['head'=8,'ctx'=64] {'ctx'}, use_global_device_ids=true, to_apply=%region_6.7 | all-reduce | flops 2064 | bytes 16512 | tf_op jit(solution)/shard_map/pmax | solution.py:39
  255.1 0.1 sub.38
  255.2 4.7 fusion
  259.9 0.1 reduce_sum.50
  259.9 0.2 fusion.21
  260.1 219.7 %all-reduce = (f32[128,16]{1,0:T(8,128)S(1)}, f32[16]{0:T(128)S(1)}) all-reduce(f32[128,16]{1,0:T(8,128)S(1)} %reduce_sum.50, f32[16]{0:T(128)S(1)} %fusion.21), channel_id=1, replica_groups=mesh['head'=8,'ctx'=64] {'ctx'}, use_global_device_ids=true, to_apply=%region_8.9 | all-reduce | flops 2064 | bytes 16512 | tf_op jit(solution)/shard_map/psum | solution.py:46
  479.9 5.7 fusion.1
  485.6 0.8 broadcast_multiply_fusion
  486.4 0.0 all-reduce.6.cloned.1.call-update
  486.5 0.0 all-reduce.10.cloned.1.call-start
  486.5 2.7 fusion.5
  489.3 174.2 %all-reduce.6.cloned.1.call-done = f32[128,1024]{1,0:T(8,128)} async-done(((f32[128,1024]{1,0:T(8,128)}), f32[128,1024]{1,0:T(8,128)}) %all-reduce.6.cloned.1.call-update) | async-done | bytes 524304 | tf_op jit(solution)/shard_map/psum | solution.py:51
  663.4 0.9 subtract_multiply_fusion
  664.4 1.8 fusion.14
  666.2 0.0 all-reduce.10.cloned.1.call-update
  666.2 0.0 all-reduce.8.cloned.1.call-start
  666.3 1.6 fusion.4
  667.8 0.0 all-reduce.8.cloned.1.call-update
  667.9 2.7 multiply_reduce_fusion
  670.5 118.5 %psum.46 = f32[16,64]{1,0:T(8,128)} all-reduce(f32[16,64]{1,0:T(8,128)S(1)} %multiply_reduce_fusion), channel_id=1, replica_groups=mesh['head'=8,'ctx'=64] {'ctx'}, use_global_device_ids=true, to_apply=%region_13.14 | all-reduce | flops 1024 | bytes 8192 | tf_op jit(solution)/shard_map/psum | solution.py:69
  789.1 0.0 all-reduce.10.cloned.1.call-done
  789.1 213.6 %all-reduce.8.cloned.1.call-done = f32[16,64,128]{2,1,0:T(8,128)} async-done(((f32[16,64,128]{2,1,0:T(8,128)}), f32[16,64,128]{2,1,0:T(8,128)}) %all-reduce.8.cloned.1.call-update) | async-done | bytes 524304 | tf_op jit(solution)/shard_map/psum | solution.py:69
  1002.6 1.9 copy.13
  1004.5 1.9 copy.14
  (2 shorter events, 0.0 us)
Async XLA Ops:
  7.2 5.3 copy-start
  7.2 5.1 copy-start.4
  7.2 656.2 %all-reduce.6.cloned.1.call-start = ((), (), s32[]{:S(2)}) async-start(), calls=%async_computation | async-start | bytes 1048576 | tf_op jit(solution)/shard_map/psum | solution.py:51
  12.5 8.3 copy-start.3
  12.5 8.4 copy-start.1
  12.5 8.4 copy-start.2
  486.5 302.6 %all-reduce.10.cloned.1.call-start = ((), (), s32[]{:S(2)}) async-start(), calls=%async_computation.2 | async-start | bytes 1048576 | tf_op jit(solution)/shard_map/psum | solution.py:70
  666.2 336.4 %all-reduce.8.cloned.1.call-start = ((), (), s32[]{:S(2)}) async-start(), calls=%async_computation.1 | async-start | bytes 1048576 | tf_op jit(solution)/shard_map/psum | solution.py:69
Sparse Core Ops, SparseCore 0:
  486.6 176.7 all-reduce.5
  666.4 75.4 all-reduce.9
  745.9 256.6 all-reduce.7
where the time goes:
time: 1020 us; the launch traced here: 1010 us
  blocking collectives  570 us (56%)
  waiting for transfers between devices  388 us (38%)
  other arithmetic  18.2 us (2%)
  matrix products  14.3 us (1%)
  between operations  13.9 us (1%)
    pmax x1, blocking collectives, shards(): main_max, index_max = lax.pmax((main_max, index_max), 'ctx')  231 us
    psum x1, blocking collectives, shards(): main_total, index_total = lax.psum((main_total, index_total), 'ctx')  220 us
    psum x1, waiting for transfers between devices, shards(): grad_query, grad_weight = lax.psum((query_part, weight_part), 'ctx')  214 us
    psum x1, waiting for transfers between devices, shards(): whole = lax.psum(jnp.sum(probs, axis=1) / total_heads, 'head')  174 us
    psum x1, blocking collectives, shards(): grad_query, grad_weight = lax.psum((query_part, weight_part), 'ctx')  119 us
  transfers between devices with their start and end apart: 3, of which 2 were waited for; matrix products, arithmetic and copies ran while one was open for 1% of the time, Pallas kernels for 0%

commit v1 on v0

v1 whole, which is shorter than its diff:
```python
import functools

import jax
import jax.numpy as jnp
from jax import lax
from jax.experimental import pallas as pl
from jax.experimental.pallas import tpu as pltpu
from jax.sharding import PartitionSpec as P

MESH = pl.DeviceIdType.MESH
LOG2E = 1.4426950408889634
score_scale = (192.0 ** -0.5) * LOG2E
loss_scale = 256.0
masked_value = -1e30


def groups_of(head_size, ctx_size):
    return head_size // 2, 4, 4, ctx_size // 16


def kernel(dims, q_ref, kt_ref, iq_ref, iw_ref, ik_ref, pos_ref, gq_ref, gw_ref, kg_ref,
           k_s, p_s, m_s, f_s, a_send, a_recv, tgt, tb_sib, tb_y, aff, wcol, lg, lg_s, u_s, qt_s,
           gq_s, gq_x, gq_l, gq_h, gw_s, gw_x, gw_l, gw_h, gw_1, gw_2, gw_f,
           kg_s, kg_sib, kg_y, send_sem, recv_sem):
    gy, gx, gl, gh = dims
    heads, depth, rows = q_ref.shape
    keys = kt_ref.shape[1]
    own = iw_ref.shape[0]
    n_own = iq_ref.shape[0]
    ih = n_own // own
    di = iq_ref.shape[1]
    kc = keys // (2 * gy)
    rx, rl, rh = n_own // gx, n_own // (gx * gl), n_own // (gx * gl * gh)
    tx = own // gx

    hd = lax.axis_index("head")
    cx = lax.axis_index("ctx")
    y, core = lax.div(hd, 2), lax.rem(hd, 2)
    x = lax.rem(cx, gx)
    zl = lax.rem(lax.div(cx, gx), gl)
    zh = lax.div(cx, gx * gl)

    def dev_x(k):
        return (hd, cx - x + lax.rem(x + k, gx))

    def dev_l(k):
        return (hd, cx - zl * gx + lax.rem(zl + k, gl) * gx)

    def dev_h(k):
        return (hd, cx - zh * (gx * gl) + lax.rem(zh + k, gh) * (gx * gl))

    def dev_y(k):
        return (lax.rem(y + k, gy) * 2 + core, cx)

    sib = (2 * y + 1 - core, cx)
    peers = ([dev_x(k) for k in range(1, gx)] + [dev_l(k) for k in range(1, gl)]
             + [dev_h(k) for k in range(1, gh)] + [dev_y(k) for k in range(1, gy)] + [sib])
    barrier = pltpu.get_barrier_semaphore()
    for peer in peers:
        pl.semaphore_signal(barrier, inc=1, device_id=peer, device_id_type=MESH)

    sems = [0]
    started = []

    def send(src, dst, device):
        i = sems[0]
        sems[0] += 1
        copy = pltpu.make_async_remote_copy(
            src_ref=src, dst_ref=dst, send_sem=send_sem.at[i], recv_sem=recv_sem.at[i],
            device_id=device, device_id_type=MESH)
        copy.start()
        started.append(copy)
        return copy

    k_s[...] = kt_ref[...].T
    base = cx * keys
    pos = pos_ref[...]

    def score_pair(p, carry):
        q2 = jnp.concatenate([q_ref[2 * p], q_ref[2 * p + 1]], axis=1)
        step = min(256, keys)
        top = jnp.full((1, 2 * rows), masked_value, jnp.float32)
        for c in range(keys // step):
            s = jnp.dot(k_s[c * step:(c + 1) * step, :], q2, preferred_element_type=jnp.float32)
            at = base + c * step + lax.broadcasted_iota(jnp.int32, (step, rows), 0)
            seen = at <= pos
            s0 = jnp.where(seen, s[:, :rows] * score_scale, masked_value)
            s1 = jnp.where(seen, s[:, rows:] * score_scale, masked_value)
            p_s[2 * p, c * step:(c + 1) * step, :] = s0
            p_s[2 * p + 1, c * step:(c + 1) * step, :] = s1
            top = jnp.maximum(top, jnp.concatenate(
                [jnp.max(s0, axis=0, keepdims=True), jnp.max(s1, axis=0, keepdims=True)], axis=1))
        for half in range(2):
            m = top[:, half * rows:(half + 1) * rows]
            total = jnp.zeros((1, rows), jnp.float32)
            for c in range(keys // step):
                e = jnp.exp2(p_s[2 * p + half, c * step:(c + 1) * step, :] - m)
                p_s[2 * p + half, c * step:(c + 1) * step, :] = e
                total = total + jnp.sum(e, axis=0, keepdims=True)
            here = head_rows == 2 * p + half
            carry = (jnp.where(here, m, carry[0]), jnp.where(here, m + jnp.log2(total), carry[1]))
        return carry

    head_rows = lax.broadcasted_iota(jnp.int32, (heads, rows), 0)
    zeros = jnp.zeros((heads, rows), jnp.float32)
    m_s[...], a_send[0, :heads, :] = lax.fori_loop(0, heads // 2, score_pair, (zeros, zeros))

    wt = iw_ref[...].astype(jnp.float32).T
    for t in range(own):
        wcol[t * ih:(t + 1) * ih, :] = jnp.broadcast_to(wt[:, t:t + 1], (ih, 128))
    qt_s[...] = iq_ref[...].T

    def logit_block(b, carry):
        start = pl.multiple_of(b * rx, rx)
        a = lax.dot_general(iq_ref[pl.ds(start, rx), :], ik_ref[...], (((1,), (1,)), ((), ())),
                            preferred_element_type=jnp.float32)
        aff[pl.ds(start, rx), :] = a
        for t in range(tx):
            w = wcol[pl.ds(pl.multiple_of(start + t * ih, ih), ih), :]
            for c in range(keys // 128):
                part = jnp.maximum(a[t * ih:(t + 1) * ih, c * 128:(c + 1) * 128], 0.0) * w
                lg_s[b, t:t + 1, c * 128:(c + 1) * 128] = jnp.sum(part, axis=0, keepdims=True)
        return carry

    lax.fori_loop(0, gx, logit_block, 0)

    diagonal = (lax.broadcasted_iota(jnp.int32, (own, 128), 1)
                == lax.broadcasted_iota(jnp.int32, (own, 128), 0))
    mine = (lax.broadcasted_iota(jnp.int32, (own, 128), 1)
            == hd * own + lax.broadcasted_iota(jnp.int32, (own, 128), 0))
    own_pos = jnp.sum(jnp.where(mine, pos.astype(jnp.float32), 0.0), axis=1, keepdims=True)
    at = (base + lax.broadcasted_iota(jnp.int32, (own, keys), 1)).astype(jnp.float32)
    logits = jnp.concatenate([lg_s[b, :tx, :] for b in range(gx)], axis=0)
    logits = jnp.where(at <= own_pos, logits * LOG2E, masked_value)
    index_max = jnp.max(logits, axis=1, keepdims=True)
    index_exp = jnp.exp2(logits - index_max)
    lg[...] = index_exp
    index_lse = index_max + jnp.log2(jnp.sum(index_exp, axis=1, keepdims=True))
    index_row = jnp.sum(jnp.where(diagonal, index_lse, 0.0), axis=0, keepdims=True)
    a_send[0, heads:, :] = jnp.broadcast_to(index_row, (8, 128))

    pl.semaphore_wait(barrier, len(peers))
    phases = [(gx, dev_x), (gl, dev_l), (gh, dev_h)]
    for i, (size, dev) in enumerate(phases):
        copies = [send(a_send.at[i], a_recv.at[i, k - 1], dev(k)) for k in range(1, size)]
        mine_lse = a_send[i]
        for copy in copies:
            copy.wait_recv()
        others = [a_recv[i, k - 1] for k in range(1, size)]
        top = functools.reduce(jnp.maximum, others, mine_lse)
        total = sum([jnp.exp2(o - top) for o in others], jnp.exp2(mine_lse - top))
        a_send[i + 1] = top + jnp.log2(total)

    f_s[...] = jnp.exp2(m_s[...] - a_send[3, :heads, :]) * (1.0 / (heads * 2 * gy))
    index_row = a_send[3, heads:heads + 1, :]
    index_all = jnp.sum(jnp.where(diagonal, index_row, 0.0), axis=1, keepdims=True)
    lg[...] = lg[...] * jnp.exp2(index_max - index_all)

    def target_block(c, carry):
        start = pl.multiple_of(c * 128, 128)
        acc = p_s[0, pl.ds(start, 128), :] * f_s[0:1, :]
        for h in range(1, heads):
            acc = acc + p_s[h, pl.ds(start, 128), :] * f_s[h:h + 1, :]
        tgt[:, pl.ds(start, 128)] = acc.T
        return carry

    lax.fori_loop(0, keys // 128, target_block, 0)

    def tgt_rows(k, which):
        return pl.ds(pl.multiple_of((lax.rem(y + k, gy) * 2 + which) * own, own), own)

    order = list(range(1, gy)) + [0]
    from_sib = [send(tgt.at[tgt_rows(k, 1 - core), :], tb_sib.at[lax.rem(y + k, gy)], sib) for k in order]
    from_y = []
    for k, copy in zip(order, from_sib):
        copy.wait_recv()
        tgt[tgt_rows(k, core), :] = tgt[tgt_rows(k, core), :] + tb_sib[lax.rem(y + k, gy)]
        if k:
            from_y.append(send(tgt.at[tgt_rows(k, core), :], tb_y.at[k - 1], dev_y(k)))
    target = tgt[tgt_rows(0, core), :]
    for i, copy in enumerate(from_y):
        copy.wait_recv()
        target = target + tb_y[i]
    grad_logits = loss_scale * (lg[...] - target)
    for b in range(gx):
        lg_s[b, :tx, :] = grad_logits[b * tx:(b + 1) * tx]

    eye = (lax.broadcasted_iota(jnp.int32, (ih, 128), 1) == lax.broadcasted_iota(jnp.int32, (ih, 128), 0))

    def grad_block(b):
        start = pl.multiple_of(b * rx, rx)
        gw_s[b] = jnp.zeros((8, 128), jnp.float32)
        for t in range(tx):
            here = pl.ds(pl.multiple_of(start + t * ih, ih), ih)
            w = wcol[here, :]
            acc = jnp.zeros((ih, 128), jnp.float32)
            for c in range(keys // 128):
                cols = slice(c * 128, (c + 1) * 128)
                g = lg_s[b, t:t + 1, cols]
                a = aff[here, cols]
                acc = acc + g * jnp.maximum(a, 0.0)
                u_s[here, cols] = jnp.where(a > 0, g * w, 0.0).astype(jnp.bfloat16)
            column = jnp.sum(acc, axis=1, keepdims=True)
            gw_s[b, t:t + 1, :] = jnp.sum(jnp.where(eye, column, 0.0), axis=0, keepdims=True)
        gq_s[pl.ds(start, rx), :] = jnp.dot(u_s[pl.ds(start, rx), :], ik_ref[...],
                                            preferred_element_type=jnp.float32)

    q_x, w_x = [], []
    for k in list(range(1, gx)) + [0]:
        b = lax.rem(x + k, gx)
        grad_block(b)
        if k:
            q_x.append(send(gq_s.at[pl.ds(pl.multiple_of(b * rx, rx), rx), :], gq_x.at[k - 1], dev_x(k)))
            w_x.append(send(gw_s.at[b], gw_x.at[k - 1], dev_x(k)))

    k_sib = []
    for k in order:
        b = lax.rem(y + k, gy)
        both = jnp.dot(qt_s[...], u_s[:, pl.ds(pl.multiple_of(b * 2 * kc, 2 * kc), 2 * kc)],
                       preferred_element_type=jnp.float32)
        kg_s[2 * b] = both[:, :kc]
        kg_s[2 * b + 1] = both[:, kc:]
        k_sib.append(send(kg_s.at[2 * b + 1 - core], kg_sib.at[b], sib))
    k_y = []
    for k, copy in zip(order, k_sib):
        b = lax.rem(y + k, gy)
        copy.wait_recv()
        kg_s[2 * b + core] = kg_s[2 * b + core] + kg_sib[b]
        if k:
            k_y.append(send(kg_s.at[2 * b + core], kg_y.at[k - 1], dev_y(k)))

    def rows_at(ref, start, size):
        return ref.at[pl.ds(pl.multiple_of(start, size), size), :]

    for copy in q_x + w_x:
        copy.wait_recv()
    at_x = x * rx
    here = pl.ds(pl.multiple_of(at_x, rx), rx)
    gq_s[here, :] = sum([gq_x[i] for i in range(gx - 1)], gq_s[here, :])
    gw_1[...] = sum([gw_x[i] for i in range(gx - 1)], gw_s[x])
    q_l, w_l = [], []
    for k in range(1, gl):
        q_l.append(send(rows_at(gq_s, at_x + lax.rem(zl + k, gl) * rl, rl), gq_l.at[k - 1], dev_l(k)))
        w_l.append(send(gw_1, gw_l.at[k - 1], dev_l(k)))

    for copy in k_y:
        copy.wait_recv()
    block = sum([kg_y[i] for i in range(gy - 1)], kg_s[hd])
    my_keys = rows_at(kg_ref, hd * kc, kc)
    kg_ref[pl.ds(pl.multiple_of(hd * kc, kc), kc), :] = block.T
    k_out = [send(my_keys, my_keys, dev_y(k)) for k in range(1, gy)]
    k_end = [send(my_keys, my_keys, sib)]

    for copy in q_l + w_l:
        copy.wait_recv()
    at_l = at_x + zl * rl
    here = pl.ds(pl.multiple_of(at_l, rl), rl)
    gq_s[here, :] = sum([gq_l[i] for i in range(gl - 1)], gq_s[here, :])
    gw_2[...] = sum([gw_l[i] for i in range(gl - 1)], gw_1[...])
    q_h, w_h = [], []
    for k in range(1, gh):
        q_h.append(send(rows_at(gq_s, at_l + lax.rem(zh + k, gh) * rh, rh), gq_h.at[k - 1], dev_h(k)))
        w_h.append(send(gw_2, gw_h.at[k - 1], dev_h(k)))

    for k, copy in enumerate(k_out, 1):
        copy.wait_recv()
        got = rows_at(kg_ref, (lax.rem(y + gy - k, gy) * 2 + core) * kc, kc)
        k_end.append(send(got, got, sib))

    for copy in q_h + w_h:
        copy.wait_recv()
    at_h = at_l + zh * rh
    here = pl.ds(pl.multiple_of(at_h, rh), rh)
    gq_ref[here, :] = sum([gq_h[i] for i in range(gh - 1)], gq_s[here, :])
    gw_f[x] = sum([gw_h[i] for i in range(gh - 1)], gw_2[...])
    out = rows_at(gq_ref, at_h, rh)
    copies = [send(out, out, dev_h(k)) for k in range(1, gh)]
    w_out = [send(gw_f.at[x], gw_f.at[x], dev_x(k)) for k in range(1, gx)]
    for copy in copies:
        copy.wait_recv()
    out = rows_at(gq_ref, at_l, rl)
    copies = [send(out, out, dev_l(k)) for k in range(1, gl)]
    for copy in copies:
        copy.wait_recv()
    out = rows_at(gq_ref, at_x, rx)
    copies = [send(out, out, dev_x(k)) for k in range(1, gx)]
    for copy in w_out:
        copy.wait_recv()
    for b in range(gx):
        gw_ref[b * tx:(b + 1) * tx, :] = gw_f[b, :tx, :ih]
    for copy in copies + k_end:
        copy.wait_recv()
    for copy in started:
        copy.wait_send()


def shards(dims, main_query, latent_keys, index_query, index_weight, index_keys, query_positions):
    gy, gx, gl, gh = dims
    rows, heads, depth = main_query.shape
    keys = latent_keys.shape[0]
    own, ih, di = index_query.shape
    n_own = own * ih
    f32 = jnp.float32
    rx, rl, rh = n_own // gx, n_own // (gx * gl), n_own // (gx * gl * gh)
    kc = keys // (2 * gy)
    n_sem = (3 * ((gx - 1) + (gl - 1) + (gh - 1))
             + 2 * (gy + gy - 1)
             + (gy - 1) + gy
             + (gh - 1) + (gl - 1) + 2 * (gx - 1))
    vmem = pl.BlockSpec(memory_space=pltpu.VMEM)
    V = pltpu.VMEM
    gq, gw, kg = pl.pallas_call(
        functools.partial(kernel, dims),
        out_shape=(jax.ShapeDtypeStruct((n_own, di), f32), jax.ShapeDtypeStruct((own, ih), f32),
                   jax.ShapeDtypeStruct((keys, di), f32)),
        in_specs=[vmem] * 6,
        out_specs=(vmem, vmem, vmem),
        scratch_shapes=[
            V((keys, depth), jnp.bfloat16),
            V((heads, keys, rows), f32),
            V((heads, rows), f32),
            V((heads, rows), f32),
            V((4, heads + 8, rows), f32),
            V((3, max(gx, gl, gh) - 1, heads + 8, rows), f32),
            V((rows, keys), f32),
            V((gy, own, keys), f32),
            V((max(gy - 1, 1), own, keys), f32),
            V((n_own, keys), f32),
            V((n_own, 128), f32),
            V((own, keys), f32),
            V((gx, 8, keys), f32),
            V((n_own, keys), jnp.bfloat16),
            V((di, n_own), jnp.bfloat16),
            V((n_own, di), f32),
            V((max(gx - 1, 1), rx, di), f32),
            V((max(gl - 1, 1), rl, di), f32),
            V((max(gh - 1, 1), rh, di), f32),
            V((gx, 8, 128), f32),
            V((max(gx - 1, 1), 8, 128), f32),
            V((max(gl - 1, 1), 8, 128), f32),
            V((max(gh - 1, 1), 8, 128), f32),
            V((8, 128), f32),
            V((8, 128), f32),
            V((gx, 8, 128), f32),
            V((2 * gy, di, kc), f32),
            V((gy, di, kc), f32),
            V((max(gy - 1, 1), di, kc), f32),
            pltpu.SemaphoreType.DMA((n_sem,)),
            pltpu.SemaphoreType.DMA((n_sem,)),
        ],
        compiler_params=pltpu.CompilerParams(
            collective_id=0, has_side_effects=True, vmem_limit_bytes=56 * 1024 * 1024),
    )(main_query.transpose(1, 2, 0), latent_keys.T, index_query.reshape(n_own, di), index_weight,
      index_keys, query_positions.reshape(1, rows))
    return gq.reshape(own, ih, di), gw, kg


def solution(mesh):
    dims = groups_of(mesh.shape["head"], mesh.shape["ctx"])
    in_specs = (
        P(None, "head", None),
        P("ctx", None),
        P("head", None, None),
        P("head", None),
        P("ctx", None),
        P(),
    )
    out_specs = (P("head", None, None), P("head", None), P("ctx", None))
    return jax.shard_map(functools.partial(shards, dims), mesh=mesh, in_specs=in_specs, out_specs=out_specs,
                         check_vma=False)
```

time: 1020 us -> 89.6 us (0.09)
  the two profiles are of different devices: /device:TPU:1 before, /device:TPU:32 now
where the time goes in v1:
time: 89.6 us; the launch traced here: 89.3 us
  Pallas kernels  83.6 us (93%)
  local copies, waits for them, and re-layouts  5.05 us (6%)
    pallas_call x1, Pallas kernels, shards(): pl.pallas_call(functools.partial(kernel, dims), out_shape=(jax.ShapeDtype...  83.6 us
    unnamed x3, local copies, waits for them, and re-layouts  5.05 us

profile of v1, /device:TPU:32, one launch (start us, length us, event | category | flops | bytes accessed | tf_op | source)
XLA Modules:
  0.0 89.3 jit_solution(17468940332062332237)
XLA Ops:
  0.6 83.6 %shard_map.85 = (f32[1024,128]{1,0:T(8,128)}, f32[16,64]{1,0:T(8,128)}, f32[1024,128]{1,0:T(8,128)}) custom-call(bf16[16,576,128]{2,1,0:T(8,128)(2,1)} %bitcast.5, bf16[576,1024]{1,0:T(8,128)(2,1)} %bitcast.6, bf16[1024,128]{1,0:T(8,128)(2,1)} %bitcast.8, bf16[16,64]{1,0:T(8,128)(2,1)} %iw_ref.1, bf16[1024,128]{1,0:T(8,128)(2,1)} %ik_ref.1, s32[1,128]{1,0:T(1,128)} %bitcast.9), custom_call_target="tpu_custom_call" | custom-call | tf_op jit(solution)/shard_map/pallas_call | solution.py:312
  84.2 1.9 %copy.12 = f32[16,64,128]{2,1,0:T(8,128)} copy(f32[16,64,128]{2,1,0:T(8,128)} %bitcast.7) | data formatting | bytes 1048576
  86.1 1.3 %copy.13 = f32[16,64]{1,0:T(8,128)} copy(f32[16,64]{1,0:T(8,128)} %get-tuple-element.13) | data formatting | bytes 8192
  87.4 1.9 %copy.14 = f32[1024,128]{1,0:T(8,128)} copy(f32[1024,128]{1,0:T(8,128)} %get-tuple-element.14) | data formatting | bytes 1048576

commit v2 on v1

--- a/solution.py
+++ b/solution.py
@@ -20,7 +20,7 @@
 
 def kernel(dims, q_ref, kt_ref, iq_ref, iw_ref, ik_ref, pos_ref, gq_ref, gw_ref, kg_ref,
            k_s, p_s, m_s, f_s, a_send, a_recv, tgt, tb_sib, tb_y, aff, wcol, lg, lg_s, u_s, qt_s,
-           gq_s, gq_x, gq_l, gq_h, gw_s, gw_x, gw_l, gw_h, gw_1, gw_2, gw_f,
+           gq_s, gq_x, gq_z, gw_s, gw_x, gw_l, gw_h, gw_1, gw_2, gw_f,
            kg_s, kg_sib, kg_y, send_sem, recv_sem):
     gy, gx, gl, gh = dims
     heads, depth, rows = q_ref.shape
@@ -30,7 +30,7 @@
     ih = n_own // own
     di = iq_ref.shape[1]
     kc = keys // (2 * gy)
-    rx, rl, rh = n_own // gx, n_own // (gx * gl), n_own // (gx * gl * gh)
+    rx, rt, rh = n_own // gx, n_own // (gx * gh), n_own // (gx * gl * gh)
     tx = own // gx
 
     hd = lax.axis_index("head")
@@ -52,9 +52,13 @@
     def dev_y(k):
         return (lax.rem(y + k, gy) * 2 + core, cx)
 
+    def dev_z(j, m):
+        return (hd, (lax.rem(zh + j, gh) * gl + lax.rem(zl + m, gl)) * gx + x)
+
+    offsets = [(j, m) for j in ((0, 1, 3, 2) if gh == 4 else range(gh)) for m in range(gl)]
     sib = (2 * y + 1 - core, cx)
-    peers = ([dev_x(k) for k in range(1, gx)] + [dev_l(k) for k in range(1, gl)]
-             + [dev_h(k) for k in range(1, gh)] + [dev_y(k) for k in range(1, gy)] + [sib])
+    peers = ([dev_x(k) for k in range(1, gx)] + [dev_z(j, m) for j, m in offsets if j or m]
+             + [dev_y(k) for k in range(1, gy)] + [sib])
     barrier = pltpu.get_barrier_semaphore()
     for peer in peers:
         pl.semaphore_signal(barrier, inc=1, device_id=peer, device_id_type=MESH)
@@ -205,12 +209,18 @@
         gq_s[pl.ds(start, rx), :] = jnp.dot(u_s[pl.ds(start, rx), :], ik_ref[...],
                                             preferred_element_type=jnp.float32)
 
-    q_x, w_x = [], []
+    def rows_at(ref, start, size):
+        return ref.at[pl.ds(pl.multiple_of(start, size), size), :]
+
+    far_first = list(dict.fromkeys(j for j, _ in reversed(offsets)))
+    q_x, w_x = [[] for _ in range(gh)], []
     for k in list(range(1, gx)) + [0]:
         b = lax.rem(x + k, gx)
         grad_block(b)
         if k:
-            q_x.append(send(gq_s.at[pl.ds(pl.multiple_of(b * rx, rx), rx), :], gq_x.at[k - 1], dev_x(k)))
+            for j in far_first:
+                q_x[j].append(send(rows_at(gq_s, b * rx + lax.rem(zh + j, gh) * rt, rt), gq_x.at[k - 1, j],
+                                   dev_x(k)))
             w_x.append(send(gw_s.at[b], gw_x.at[k - 1], dev_x(k)))
 
     k_sib = []
@@ -229,19 +239,22 @@
         if k:
             k_y.append(send(kg_s.at[2 * b + core], kg_y.at[k - 1], dev_y(k)))
 
-    def rows_at(ref, start, size):
-        return ref.at[pl.ds(pl.multiple_of(start, size), size), :]
-
-    for copy in q_x + w_x:
-        copy.wait_recv()
     at_x = x * rx
-    here = pl.ds(pl.multiple_of(at_x, rx), rx)
-    gq_s[here, :] = sum([gq_x[i] for i in range(gx - 1)], gq_s[here, :])
+    q_z = []
+    for j in far_first:
+        for copy in q_x[j]:
+            copy.wait_recv()
+        first = at_x + lax.rem(zh + j, gh) * rt
+        here = pl.ds(pl.multiple_of(first, rt), rt)
+        gq_s[here, :] = sum([gq_x[i, j] for i in range(gx - 1)], gq_s[here, :])
+        for m in range(gl):
+            if j or m:
+                q_z.append(send(rows_at(gq_s, first + lax.rem(zl + m, gl) * rh, rh), gq_z.at[j * gl + m],
+                                dev_z(j, m)))
+    for copy in w_x:
+        copy.wait_recv()
     gw_1[...] = sum([gw_x[i] for i in range(gx - 1)], gw_s[x])
-    q_l, w_l = [], []
-    for k in range(1, gl):
-        q_l.append(send(rows_at(gq_s, at_x + lax.rem(zl + k, gl) * rl, rl), gq_l.at[k - 1], dev_l(k)))
-        w_l.append(send(gw_1, gw_l.at[k - 1], dev_l(k)))
+    w_l = [send(gw_1, gw_l.at[k - 1], dev_z(0, k)) for k in range(1, gl)]
 
     for copy in k_y:
         copy.wait_recv()
@@ -251,47 +264,50 @@
     k_out = [send(my_keys, my_keys, dev_y(k)) for k in range(1, gy)]
     k_end = [send(my_keys, my_keys, sib)]
 
-    for copy in q_l + w_l:
-        copy.wait_recv()
-    at_l = at_x + zl * rl
-    here = pl.ds(pl.multiple_of(at_l, rl), rl)
-    gq_s[here, :] = sum([gq_l[i] for i in range(gl - 1)], gq_s[here, :])
+    for copy in w_l:
+        copy.wait_recv()
     gw_2[...] = sum([gw_l[i] for i in range(gl - 1)], gw_1[...])
-    q_h, w_h = [], []
-    for k in range(1, gh):
-        q_h.append(send(rows_at(gq_s, at_l + lax.rem(zh + k, gh) * rh, rh), gq_h.at[k - 1], dev_h(k)))
-        w_h.append(send(gw_2, gw_h.at[k - 1], dev_h(k)))
+    w_h = [send(gw_2, gw_h.at[k - 1], dev_z(k, 0)) for k in range(1, gh)]
+
+    for copy in q_z:
+        copy.wait_recv()
+    first = at_x + zh * rt + zl * rh
+    here = pl.ds(pl.multiple_of(first, rh), rh)
+    gq_ref[here, :] = sum([gq_z[i] for i in range(1, gl * gh)], gq_s[here, :])
+    out = rows_at(gq_ref, first, rh)
+    back_z = {(j, m): send(out, out, dev_z(j, m)) for j, m in offsets if j or m}
 
     for k, copy in enumerate(k_out, 1):
         copy.wait_recv()
         got = rows_at(kg_ref, (lax.rem(y + gy - k, gy) * 2 + core) * kc, kc)
         k_end.append(send(got, got, sib))
 
-    for copy in q_h + w_h:
-        copy.wait_recv()
-    at_h = at_l + zh * rh
-    here = pl.ds(pl.multiple_of(at_h, rh), rh)
-    gq_ref[here, :] = sum([gq_h[i] for i in range(gh - 1)], gq_s[here, :])
+    for copy in w_h:
+        copy.wait_recv()
     gw_f[x] = sum([gw_h[i] for i in range(gh - 1)], gw_2[...])
-    out = rows_at(gq_ref, at_h, rh)
-    copies = [send(out, out, dev_h(k)) for k in range(1, gh)]
     w_out = [send(gw_f.at[x], gw_f.at[x], dev_x(k)) for k in range(1, gx)]
-    for copy in copies:
-        copy.wait_recv()
-    out = rows_at(gq_ref, at_l, rl)
-    copies = [send(out, out, dev_l(k)) for k in range(1, gl)]
-    for copy in copies:
-        copy.wait_recv()
-    out = rows_at(gq_ref, at_x, rx)
-    copies = [send(out, out, dev_x(k)) for k in range(1, gx)]
+
+    back_x = []
+    for j in reversed(far_first):
+        for m in range(gl):
+            if j or m:
+                back_z[j, m].wait_recv()
+        out = rows_at(gq_ref, at_x + lax.rem(zh + gh - j, gh) * rt, rt)
+        back_x += [send(out, out, dev_x(k)) for k in range(1, gx)]
     for copy in w_out:
         copy.wait_recv()
     for b in range(gx):
         gw_ref[b * tx:(b + 1) * tx, :] = gw_f[b, :tx, :ih]
-    for copy in copies + k_end:
+    for copy in back_x + k_end:
         copy.wait_recv()
     for copy in started:
         copy.wait_send()
+
+
+def copy_kernel(gq_ref, gw_ref, kg_ref, gq_out, gw_out, kg_out):
+    gq_out[...] = gq_ref[...]
+    gw_out[...] = gw_ref[...]
+    kg_out[...] = kg_ref[...]
 
 
 def shards(dims, main_query, latent_keys, index_query, index_weight, index_keys, query_positions):
@@ -301,12 +317,12 @@
     own, ih, di = index_query.shape
     n_own = own * ih
     f32 = jnp.float32
-    rx, rl, rh = n_own // gx, n_own // (gx * gl), n_own // (gx * gl * gh)
+    rx, rt, rh = n_own // gx, n_own // (gx * gh), n_own // (gx * gl * gh)
     kc = keys // (2 * gy)
-    n_sem = (3 * ((gx - 1) + (gl - 1) + (gh - 1))
+    n_sem = (2 * ((gx - 1) + (gl - 1) + (gh - 1))
              + 2 * (gy + gy - 1)
-             + (gy - 1) + gy
-             + (gh - 1) + (gl - 1) + 2 * (gx - 1))
+             + (gy - 1) + gy + gx - 1
+             + 2 * ((gx - 1) * gh + gl * gh - 1))
     vmem = pl.BlockSpec(memory_space=pltpu.VMEM)
     V = pltpu.VMEM
     gq, gw, kg = pl.pallas_call(
@@ -332,9 +348,8 @@
             V((n_own, keys), jnp.bfloat16),
             V((di, n_own), jnp.bfloat16),
             V((n_own, di), f32),
-            V((max(gx - 1, 1), rx, di), f32),
-            V((max(gl - 1, 1), rl, di), f32),
-            V((max(gh - 1, 1), rh, di), f32),
+            V((max(gx - 1, 1), gh, rt, di), f32),
+            V((gl * gh, rh, di), f32),
             V((gx, 8, 128), f32),
             V((max(gx - 1, 1), 8, 128), f32),
             V((max(gl - 1, 1), 8, 128), f32),
@@ -349,9 +364,17 @@
             pltpu.SemaphoreType.DMA((n_sem,)),
         ],
         compiler_params=pltpu.CompilerParams(
-            collective_id=0, has_side_effects=True, vmem_limit_bytes=56 * 1024 * 1024),
+            collective_id=0, has_side_effects=True, vmem_limit_bytes=40 * 1024 * 1024),
     )(main_query.transpose(1, 2, 0), latent_keys.T, index_query.reshape(n_own, di), index_weight,
       index_keys, query_positions.reshape(1, rows))
+    gq, gw, kg = pl.pallas_call(
+        copy_kernel,
+        out_shape=(jax.ShapeDtypeStruct((n_own, di), f32), jax.ShapeDtypeStruct((own, ih), f32),
+                   jax.ShapeDtypeStruct((keys, di), f32)),
+        in_specs=[vmem] * 3,
+        out_specs=(vmem,) * 3,
+        compiler_params=pltpu.CompilerParams(vmem_limit_bytes=8 * 1024 * 1024),
+    )(gq, gw, kg)
     return gq.reshape(own, ih, di), gw, kg
 
 

time: 89.6 us -> 82.5 us (0.921)
  the two profiles are of different devices: /device:TPU:32 before, /device:TPU:1 now
where the time goes in v2:
time: 82.5 us; the launch traced here: 82.2 us
  Pallas kernels  75.4 us (91%)
  local copies, waits for them, and re-layouts  6.17 us (7%)
    pallas_call x1, Pallas kernels, shards(): pl.pallas_call(functools.partial(kernel, dims), out_shape=(jax.ShapeDtype...  74.4 us
    unnamed x12, local copies, waits for them, and re-layouts  6.17 us

profile of v2, /device:TPU:1, one launch (start us, length us, event | category | flops | bytes accessed | tf_op | source)
XLA Modules:
  0.0 82.2 jit_solution(11547764942571427564)
XLA Ops:
  0.6 0.0 copy-start
  0.6 1.7 %copy-done = bf16[128,16,576]{0,2,1:T(8,128)(2,1)S(1)} copy-done((bf16[128,16,576]{0,2,1:T(8,128)(2,1)S(1)}, bf16[128,16,576]{0,2,1:T(8,128)(2,1)}, u32[]{:S(2)}) %copy-start) | copy-done | bytes 2359320
  2.3 0.0 copy-start.1
  2.3 1.3 %copy-done.1 = bf16[1024,576]{0,1:T(8,128)(2,1)S(1)} copy-done((bf16[1024,576]{0,1:T(8,128)(2,1)S(1)}, bf16[1024,576]{0,1:T(8,128)(2,1)}, u32[]{:S(2)}) %copy-start.1) | copy-done | bytes 1179672
  3.6 0.0 copy-start.2
  3.6 0.9 %copy-done.2 = bf16[16,64,128]{2,1,0:T(8,128)(2,1)S(1)} copy-done((bf16[16,64,128]{2,1,0:T(8,128)(2,1)S(1)}, bf16[16,64,128]{2,1,0:T(8,128)(2,1)}, u32[]{:S(2)}) %copy-start.2) | copy-done | bytes 262168
  4.5 0.0 copy-start.3
  4.5 0.9 %copy-done.3 = bf16[1024,128]{1,0:T(8,128)(2,1)S(1)} copy-done((bf16[1024,128]{1,0:T(8,128)(2,1)S(1)}, bf16[1024,128]{1,0:T(8,128)(2,1)}, u32[]{:S(2)}) %copy-start.3) | copy-done | bytes 262168
  5.5 0.0 copy-start.4
  5.5 0.7 copy-done.4
  6.2 0.0 copy-start.5
  6.2 0.7 copy-done.5
  6.8 74.4 %shard_map.85 = (f32[1024,128]{1,0:T(8,128)S(1)}, f32[16,64]{1,0:T(8,128)S(1)}, f32[1024,128]{1,0:T(8,128)S(1)}) custom-call(bf16[16,576,128]{2,1,0:T(8,128)(2,1)S(1)} %bitcast.5, bf16[576,1024]{1,0:T(8,128)(2,1)S(1)} %bitcast.6, bf16[1024,128]{1,0:T(8,128)(2,1)S(1)} %bitcast.7, bf16[16,64]{1,0:T(8,128)(2,1)S(1)} %copy-done.4, ...), custom_call_target="tpu_custom_call" | custom-call | tf_op jit(solution)/shard_map/pallas_call | solution.py:328
  81.2 1.0 %shard_map.86 = (f32[1024,128]{1,0:T(8,128)}, f32[16,64]{1,0:T(8,128)}, f32[1024,128]{1,0:T(8,128)}) custom-call(f32[1024,128]{1,0:T(8,128)S(1)} %get-tuple-element.9.gq_ref, f32[16,64]{1,0:T(8,128)S(1)} %get-tuple-element.10.gw_ref, f32[1024,128]{1,0:T(8,128)S(1)} %get-tuple-element.11.kg_ref), custom_call_target="tpu_custom_call" | custom-call | tf_op jit(solution)/shard_map/pallas_call | solution.py:370
Async XLA Ops:
  0.6 1.7 %copy-start = (bf16[128,16,576]{0,2,1:T(8,128)(2,1)S(1)}, bf16[128,16,576]{0,2,1:T(8,128)(2,1)}, u32[]{:S(2)}) copy-start(bf16[128,16,576]{0,2,1:T(8,128)(2,1)} %param.6) | copy-start | bytes 7077892
  2.3 1.3 %copy-start.1 = (bf16[1024,576]{0,1:T(8,128)(2,1)S(1)}, bf16[1024,576]{0,1:T(8,128)(2,1)}, u32[]{:S(2)}) copy-start(bf16[1024,576]{0,1:T(8,128)(2,1)} %param.7) | copy-start | bytes 3538948
  3.6 0.9 %copy-start.2 = (bf16[16,64,128]{2,1,0:T(8,128)(2,1)S(1)}, bf16[16,64,128]{2,1,0:T(8,128)(2,1)}, u32[]{:S(2)}) copy-start(bf16[16,64,128]{2,1,0:T(8,128)(2,1)} %param.8) | copy-start | bytes 786436
  4.5 0.9 %copy-start.3 = (bf16[1024,128]{1,0:T(8,128)(2,1)S(1)}, bf16[1024,128]{1,0:T(8,128)(2,1)}, u32[]{:S(2)}) copy-start(bf16[1024,128]{1,0:T(8,128)(2,1)} %ik_ref.1) | copy-start | bytes 786436
  5.5 0.7 copy-start.4
  6.2 0.7 copy-start.5

commit v3 on v2

--- a/solution.py
+++ b/solution.py
@@ -18,8 +18,9 @@
     return head_size // 2, 4, 4, ctx_size // 16
 
 
-def kernel(dims, q_ref, kt_ref, iq_ref, iw_ref, ik_ref, pos_ref, gq_ref, gw_ref, kg_ref,
-           k_s, p_s, m_s, f_s, a_send, a_recv, tgt, tb_sib, tb_y, aff, wcol, lg, lg_s, u_s, qt_s,
+def kernel(dims, q_in, kt_in, iq_in, iw_in, ik_in, pos_in, gq_ref, gw_ref, kg_ref,
+           q_ref, kt_ref, iq_ref, ik_ref, iw_ref, pos_ref, in_sem,
+           k_s, p_s, m_s, f_s, a_send, a_recv, i_send, i_recv, tgt, tb_sib, tb_y, aff, wcol, lg, lg_s, u_s, qt_s,
            gq_s, gq_x, gq_z, gw_s, gw_x, gw_l, gw_h, gw_1, gw_2, gw_f,
            kg_s, kg_sib, kg_y, send_sem, recv_sem):
     gy, gx, gl, gh = dims
@@ -43,12 +44,6 @@
     def dev_x(k):
         return (hd, cx - x + lax.rem(x + k, gx))
 
-    def dev_l(k):
-        return (hd, cx - zl * gx + lax.rem(zl + k, gl) * gx)
-
-    def dev_h(k):
-        return (hd, cx - zh * (gx * gl) + lax.rem(zh + k, gh) * (gx * gl))
-
     def dev_y(k):
         return (lax.rem(y + k, gy) * 2 + core, cx)
 
@@ -62,6 +57,24 @@
     barrier = pltpu.get_barrier_semaphore()
     for peer in peers:
         pl.semaphore_signal(barrier, inc=1, device_id=peer, device_id_type=MESH)
+
+    group = max(heads // 4, 2)
+
+    def load_heads(g):
+        part = pl.ds(g * group, group)
+        return pltpu.make_async_copy(q_in.at[part], q_ref.at[part], in_sem.at[5 + g])
+
+    load_keys = pltpu.make_async_copy(kt_in, kt_ref, in_sem.at[0])
+    load_index = [pltpu.make_async_copy(iq_in, iq_ref, in_sem.at[1]),
+                  pltpu.make_async_copy(ik_in, ik_ref, in_sem.at[2]),
+                  pltpu.make_async_copy(iw_in, iw_ref, in_sem.at[3])]
+    load_positions = pltpu.make_async_copy(pos_in, pos_ref, in_sem.at[4])
+    load_keys.start()
+    load_positions.start()
+    for g in range(heads // group):
+        load_heads(g).start()
+    for copy in load_index:
+        copy.start()
 
     sems = [0]
     started = []
@@ -76,6 +89,8 @@
         started.append(copy)
         return copy
 
+    load_keys.wait()
+    load_positions.wait()
     k_s[...] = kt_ref[...].T
     base = cx * keys
     pos = pos_ref[...]
@@ -107,8 +122,35 @@
 
     head_rows = lax.broadcasted_iota(jnp.int32, (heads, rows), 0)
     zeros = jnp.zeros((heads, rows), jnp.float32)
-    m_s[...], a_send[0, :heads, :] = lax.fori_loop(0, heads // 2, score_pair, (zeros, zeros))
-
+
+    def score_group(g, carry):
+        load_heads(g).wait()
+        for i in range(group // 2):
+            carry = score_pair(g * (group // 2) + i, carry)
+        return carry
+
+    m_s[...], a_send[0] = lax.fori_loop(0, heads // group, score_group, (zeros, zeros))
+
+    phases = [(gx, dev_x), (gl, lambda k: dev_z(0, k)), (gh, lambda k: dev_z(k, 0))]
+
+    def share(i, buf, got):
+        size, dev = phases[i]
+        return [send(buf.at[i], got.at[i, k - 1], dev(k)) for k in range(1, size)]
+
+    def combine(i, buf, got, copies):
+        for copy in copies:
+            copy.wait_recv()
+        mine_lse = buf[i]
+        others = [got[i, k] for k in range(len(copies))]
+        top = functools.reduce(jnp.maximum, others, mine_lse)
+        total = sum([jnp.exp2(o - top) for o in others], jnp.exp2(mine_lse - top))
+        buf[i + 1] = top + jnp.log2(total)
+
+    pl.semaphore_wait(barrier, len(peers))
+    main = share(0, a_send, a_recv)
+
+    for copy in load_index:
+        copy.wait()
     wt = iw_ref[...].astype(jnp.float32).T
     for t in range(own):
         wcol[t * ih:(t + 1) * ih, :] = jnp.broadcast_to(wt[:, t:t + 1], (ih, 128))
@@ -141,25 +183,18 @@
     lg[...] = index_exp
     index_lse = index_max + jnp.log2(jnp.sum(index_exp, axis=1, keepdims=True))
     index_row = jnp.sum(jnp.where(diagonal, index_lse, 0.0), axis=0, keepdims=True)
-    a_send[0, heads:, :] = jnp.broadcast_to(index_row, (8, 128))
-
-    pl.semaphore_wait(barrier, len(peers))
-    phases = [(gx, dev_x), (gl, dev_l), (gh, dev_h)]
-    for i, (size, dev) in enumerate(phases):
-        copies = [send(a_send.at[i], a_recv.at[i, k - 1], dev(k)) for k in range(1, size)]
-        mine_lse = a_send[i]
-        for copy in copies:
-            copy.wait_recv()
-        others = [a_recv[i, k - 1] for k in range(1, size)]
-        top = functools.reduce(jnp.maximum, others, mine_lse)
-        total = sum([jnp.exp2(o - top) for o in others], jnp.exp2(mine_lse - top))
-        a_send[i + 1] = top + jnp.log2(total)
-
-    f_s[...] = jnp.exp2(m_s[...] - a_send[3, :heads, :]) * (1.0 / (heads * 2 * gy))
-    index_row = a_send[3, heads:heads + 1, :]
-    index_all = jnp.sum(jnp.where(diagonal, index_row, 0.0), axis=1, keepdims=True)
-    lg[...] = lg[...] * jnp.exp2(index_max - index_all)
-
+    i_send[0] = jnp.broadcast_to(index_row, (8, 128))
+
+    combine(0, a_send, a_recv, main)
+    main = share(1, a_send, a_recv)
+    index = share(0, i_send, i_recv)
+    combine(1, a_send, a_recv, main)
+    main = share(2, a_send, a_recv)
+    combine(0, i_send, i_recv, index)
+    index = share(1, i_send, i_recv)
+    combine(2, a_send, a_recv, main)
+
+    f_s[...] = jnp.exp2(m_s[...] - a_send[3]) * (1.0 / (heads * 2 * gy))
     def target_block(c, carry):
         start = pl.multiple_of(c * 128, 128)
         acc = p_s[0, pl.ds(start, 128), :] * f_s[0:1, :]
@@ -176,11 +211,16 @@
     order = list(range(1, gy)) + [0]
     from_sib = [send(tgt.at[tgt_rows(k, 1 - core), :], tb_sib.at[lax.rem(y + k, gy)], sib) for k in order]
     from_y = []
+    combine(1, i_send, i_recv, index)
+    index = share(2, i_send, i_recv)
     for k, copy in zip(order, from_sib):
         copy.wait_recv()
         tgt[tgt_rows(k, core), :] = tgt[tgt_rows(k, core), :] + tb_sib[lax.rem(y + k, gy)]
         if k:
             from_y.append(send(tgt.at[tgt_rows(k, core), :], tb_y.at[k - 1], dev_y(k)))
+    combine(2, i_send, i_recv, index)
+    index_all = jnp.sum(jnp.where(diagonal, i_send[3, 0:1, :], 0.0), axis=1, keepdims=True)
+    lg[...] = lg[...] * jnp.exp2(index_max - index_all)
     target = tgt[tgt_rows(0, core), :]
     for i, copy in enumerate(from_y):
         copy.wait_recv()
@@ -319,25 +359,35 @@
     f32 = jnp.float32
     rx, rt, rh = n_own // gx, n_own // (gx * gh), n_own // (gx * gl * gh)
     kc = keys // (2 * gy)
-    n_sem = (2 * ((gx - 1) + (gl - 1) + (gh - 1))
+    n_sem = (3 * ((gx - 1) + (gl - 1) + (gh - 1))
              + 2 * (gy + gy - 1)
              + (gy - 1) + gy + gx - 1
              + 2 * ((gx - 1) * gh + gl * gh - 1))
     vmem = pl.BlockSpec(memory_space=pltpu.VMEM)
+    hbm = pl.BlockSpec(memory_space=pltpu.HBM)
     V = pltpu.VMEM
     gq, gw, kg = pl.pallas_call(
         functools.partial(kernel, dims),
         out_shape=(jax.ShapeDtypeStruct((n_own, di), f32), jax.ShapeDtypeStruct((own, ih), f32),
                    jax.ShapeDtypeStruct((keys, di), f32)),
-        in_specs=[vmem] * 6,
+        in_specs=[hbm] * 6,
         out_specs=(vmem, vmem, vmem),
         scratch_shapes=[
+            V((heads, depth, rows), jnp.bfloat16),
+            V((depth, keys), jnp.bfloat16),
+            V((n_own, di), jnp.bfloat16),
+            V((keys, di), jnp.bfloat16),
+            V((own, ih), jnp.bfloat16),
+            V((1, rows), jnp.int32),
+            pltpu.SemaphoreType.DMA((9,)),
             V((keys, depth), jnp.bfloat16),
             V((heads, keys, rows), f32),
             V((heads, rows), f32),
             V((heads, rows), f32),
-            V((4, heads + 8, rows), f32),
-            V((3, max(gx, gl, gh) - 1, heads + 8, rows), f32),
+            V((4, heads, rows), f32),
+            V((3, max(gx, gl, gh) - 1, heads, rows), f32),
+            V((4, 8, 128), f32),
+            V((3, max(gx, gl, gh) - 1, 8, 128), f32),
             V((rows, keys), f32),
             V((gy, own, keys), f32),
             V((max(gy - 1, 1), own, keys), f32),
@@ -364,9 +414,10 @@
             pltpu.SemaphoreType.DMA((n_sem,)),
         ],
         compiler_params=pltpu.CompilerParams(
-            collective_id=0, has_side_effects=True, vmem_limit_bytes=40 * 1024 * 1024),
-    )(main_query.transpose(1, 2, 0), latent_keys.T, index_query.reshape(n_own, di), index_weight,
-      index_keys, query_positions.reshape(1, rows))
+            collective_id=0, has_side_effects=True, vmem_limit_bytes=48 * 1024 * 1024),
+    )(*[pltpu.with_memory_space_constraint(v, pltpu.HBM) for v in (
+        main_query.transpose(1, 2, 0), latent_keys.T, index_query.reshape(n_own, di), index_weight,
+        index_keys, query_positions.reshape(1, rows))])
     gq, gw, kg = pl.pallas_call(
         copy_kernel,
         out_shape=(jax.ShapeDtypeStruct((n_own, di), f32), jax.ShapeDtypeStruct((own, ih), f32),

time: 82.5 us -> 73.4 us (0.89)
  local copies, waits for them, and re-layouts: 6.17 us -> 0 us
  Pallas kernels: 75.4 us -> 72.7 us
    unnamed x12 -> x0, local copies, waits for them, and re-layouts: 6.17 us -> none
    pallas_call x1, Pallas kernels: 74.4 us -> 71.7 us  [shards(): pl.pallas_call(functools.partial(kernel, dims), out_shape=(jax.ShapeDtype...]
where the time goes in v3:
time: 73.4 us; the launch traced here: 73.3 us
  Pallas kernels  72.7 us (99%)
    pallas_call x1, Pallas kernels, shards(): pl.pallas_call(functools.partial(kernel, dims), out_shape=(jax.ShapeDtype...  71.7 us

profile of v3, /device:TPU:1, one launch (start us, length us, event | category | flops | bytes accessed | tf_op | source)
XLA Modules:
  0.0 73.3 jit_solution(4809497098197033635)
XLA Ops:
  0.6 71.7 %shard_map.85 = (f32[1024,128]{1,0:T(8,128)S(1)}, f32[16,64]{1,0:T(8,128)S(1)}, f32[1024,128]{1,0:T(8,128)S(1)}) custom-call(bf16[16,576,128]{2,1,0:T(8,128)(2,1)} %bitcast.5, bf16[576,1024]{1,0:T(8,128)(2,1)} %bitcast.6, bf16[1024,128]{1,0:T(8,128)(2,1)} %bitcast.7, bf16[16,64]{1,0:T(8,128)(2,1)} %iw_in.1, bf16[1024,128]{1,0:T(8,128)(2,1)} %ik_in.1, ...), custom_call_target="tpu_custom_call" | custom-call | tf_op jit(solution)/shard_map/pallas_call | solution.py:369
  72.3 1.0 %shard_map.86 = (f32[1024,128]{1,0:T(8,128)}, f32[16,64]{1,0:T(8,128)}, f32[1024,128]{1,0:T(8,128)}) custom-call(f32[1024,128]{1,0:T(8,128)S(1)} %get-tuple-element.9.gq_ref, f32[16,64]{1,0:T(8,128)S(1)} %get-tuple-element.10.gw_ref, f32[1024,128]{1,0:T(8,128)S(1)} %get-tuple-element.11.kg_ref), custom_call_target="tpu_custom_call" | custom-call | tf_op jit(solution)/shard_map/pallas_call | solution.py:421

commit v4 on v3

--- a/solution.py
+++ b/solution.py
@@ -195,39 +195,56 @@
     combine(2, a_send, a_recv, main)
 
     f_s[...] = jnp.exp2(m_s[...] - a_send[3]) * (1.0 / (heads * 2 * gy))
-    def target_block(c, carry):
-        start = pl.multiple_of(c * 128, 128)
+    def target_block(f, c, carry):
+        start = pl.multiple_of(f * part + c * 128, 128)
         acc = p_s[0, pl.ds(start, 128), :] * f_s[0:1, :]
         for h in range(1, heads):
             acc = acc + p_s[h, pl.ds(start, 128), :] * f_s[h:h + 1, :]
-        tgt[:, pl.ds(start, 128)] = acc.T
+        block = acc.T
+        cols = pl.ds(pl.multiple_of(c * 128, 128), 128)
+        for d in range(2 * gy):
+            for g in range(gx):
+                first = d * own + g * tx
+                tgt[d, g, f * tx:(f + 1) * tx, cols] = block[first:first + tx]
         return carry
 
-    lax.fori_loop(0, keys // 128, target_block, 0)
-
-    def tgt_rows(k, which):
-        return pl.ds(pl.multiple_of((lax.rem(y + k, gy) * 2 + which) * own, own), own)
+    fold = 8 // tx
+    part = keys // fold
+    for f in range(fold):
+        lax.fori_loop(0, part // 128, functools.partial(target_block, f), 0)
 
     order = list(range(1, gy)) + [0]
-    from_sib = [send(tgt.at[tgt_rows(k, 1 - core), :], tb_sib.at[lax.rem(y + k, gy)], sib) for k in order]
-    from_y = []
+    row_groups = [lax.rem(x + k, gx) for k in list(range(1, gx)) + [0]]
+
+    def head_at(k, which):
+        return lax.rem(y + k, gy) * 2 + which
+
+    from_sib = [[send(tgt.at[head_at(k, 1 - core), g], tb_sib.at[lax.rem(y + k, gy), g], sib) for k in order]
+                for g in row_groups]
     combine(1, i_send, i_recv, index)
     index = share(2, i_send, i_recv)
-    for k, copy in zip(order, from_sib):
-        copy.wait_recv()
-        tgt[tgt_rows(k, core), :] = tgt[tgt_rows(k, core), :] + tb_sib[lax.rem(y + k, gy)]
-        if k:
-            from_y.append(send(tgt.at[tgt_rows(k, core), :], tb_y.at[k - 1], dev_y(k)))
+    from_y = []
+    for g, copies in zip(row_groups, from_sib):
+        from_y.append([])
+        for k, copy in zip(order, copies):
+            copy.wait_recv()
+            here = head_at(k, core)
+            tgt[here, g] = tgt[here, g] + tb_sib[lax.rem(y + k, gy), g]
+            if k:
+                from_y[-1].append(send(tgt.at[here, g], tb_y.at[k - 1, g], dev_y(k)))
     combine(2, i_send, i_recv, index)
     index_all = jnp.sum(jnp.where(diagonal, i_send[3, 0:1, :], 0.0), axis=1, keepdims=True)
-    lg[...] = lg[...] * jnp.exp2(index_max - index_all)
-    target = tgt[tgt_rows(0, core), :]
-    for i, copy in enumerate(from_y):
-        copy.wait_recv()
-        target = target + tb_y[i]
-    grad_logits = loss_scale * (lg[...] - target)
+    index_probs = lg[...] * jnp.exp2(index_max - index_all)
     for b in range(gx):
-        lg_s[b, :tx, :] = grad_logits[b * tx:(b + 1) * tx]
+        lg_s[b, :tx, :] = index_probs[b * tx:(b + 1) * tx]
+
+    def grad_logits(b, copies):
+        for copy in copies:
+            copy.wait_recv()
+        target = sum([tb_y[i, b] for i in range(gy - 1)], tgt[hd, b])
+        for f in range(fold):
+            cols = slice(f * part, (f + 1) * part)
+            lg_s[b, :tx, cols] = loss_scale * (lg_s[b, :tx, cols] - target[f * tx:(f + 1) * tx])
 
     eye = (lax.broadcasted_iota(jnp.int32, (ih, 128), 1) == lax.broadcasted_iota(jnp.int32, (ih, 128), 0))
 
@@ -254,8 +271,8 @@
 
     far_first = list(dict.fromkeys(j for j, _ in reversed(offsets)))
     q_x, w_x = [[] for _ in range(gh)], []
-    for k in list(range(1, gx)) + [0]:
-        b = lax.rem(x + k, gx)
+    for k, b, copies in zip(list(range(1, gx)) + [0], row_groups, from_y):
+        grad_logits(b, copies)
         grad_block(b)
         if k:
             for j in far_first:
@@ -359,8 +376,9 @@
     f32 = jnp.float32
     rx, rt, rh = n_own // gx, n_own // (gx * gh), n_own // (gx * gl * gh)
     kc = keys // (2 * gy)
+    tx = own // gx
     n_sem = (3 * ((gx - 1) + (gl - 1) + (gh - 1))
-             + 2 * (gy + gy - 1)
+             + (gx + 1) * (gy + gy - 1)
              + (gy - 1) + gy + gx - 1
              + 2 * ((gx - 1) * gh + gl * gh - 1))
     vmem = pl.BlockSpec(memory_space=pltpu.VMEM)
@@ -388,9 +406,9 @@
             V((3, max(gx, gl, gh) - 1, heads, rows), f32),
             V((4, 8, 128), f32),
             V((3, max(gx, gl, gh) - 1, 8, 128), f32),
-            V((rows, keys), f32),
-            V((gy, own, keys), f32),
-            V((max(gy - 1, 1), own, keys), f32),
+            V((2 * gy, gx, 8, keys * tx // 8), f32),
+            V((gy, gx, 8, keys * tx // 8), f32),
+            V((max(gy - 1, 1), gx, 8, keys * tx // 8), f32),
             V((n_own, keys), f32),
             V((n_own, 128), f32),
             V((own, keys), f32),

time: 73.4 us -> 72.9 us (level)
  no operation moved by 1% of the time
where the time goes in v4:
time: 72.9 us; the launch traced here: 72.8 us
  Pallas kernels  72.1 us (99%)
    pallas_call x1, Pallas kernels, shards(): pl.pallas_call(functools.partial(kernel, dims), out_shape=(jax.ShapeDtype...  71.1 us

profile of v4, /device:TPU:1, one launch (start us, length us, event | category | flops | bytes accessed | tf_op | source)
XLA Modules:
  0.0 72.8 jit_solution(619776132770513270)
XLA Ops:
  0.6 71.1 %shard_map.85 = (f32[1024,128]{1,0:T(8,128)S(1)}, f32[16,64]{1,0:T(8,128)S(1)}, f32[1024,128]{1,0:T(8,128)S(1)}) custom-call(bf16[16,576,128]{2,1,0:T(8,128)(2,1)} %bitcast.5, bf16[576,1024]{1,0:T(8,128)(2,1)} %bitcast.6, bf16[1024,128]{1,0:T(8,128)(2,1)} %bitcast.7, bf16[16,64]{1,0:T(8,128)(2,1)} %iw_in.1, bf16[1024,128]{1,0:T(8,128)(2,1)} %ik_in.1, ...), custom_call_target="tpu_custom_call" | custom-call | tf_op jit(solution)/shard_map/pallas_call | solution.py:387
  71.7 1.0 %shard_map.86 = (f32[1024,128]{1,0:T(8,128)}, f32[16,64]{1,0:T(8,128)}, f32[1024,128]{1,0:T(8,128)}) custom-call(f32[1024,128]{1,0:T(8,128)S(1)} %get-tuple-element.9.gq_ref, f32[16,64]{1,0:T(8,128)S(1)} %get-tuple-element.10.gw_ref, f32[1024,128]{1,0:T(8,128)S(1)} %get-tuple-element.11.kg_ref), custom_call_target="tpu_custom_call" | custom-call | tf_op jit(solution)/shard_map/pallas_call | solution.py:439

commit v5 on v4

--- a/solution.py
+++ b/solution.py
@@ -54,10 +54,6 @@
     sib = (2 * y + 1 - core, cx)
     peers = ([dev_x(k) for k in range(1, gx)] + [dev_z(j, m) for j, m in offsets if j or m]
              + [dev_y(k) for k in range(1, gy)] + [sib])
-    barrier = pltpu.get_barrier_semaphore()
-    for peer in peers:
-        pl.semaphore_signal(barrier, inc=1, device_id=peer, device_id_type=MESH)
-
     group = max(heads // 4, 2)
 
     def load_heads(g):
@@ -75,6 +71,10 @@
         load_heads(g).start()
     for copy in load_index:
         copy.start()
+
+    barrier = pltpu.get_barrier_semaphore()
+    for peer in peers:
+        pl.semaphore_signal(barrier, inc=1, device_id=peer, device_id_type=MESH)
 
     sems = [0]
     started = []
@@ -344,6 +344,9 @@
     gw_f[x] = sum([gw_h[i] for i in range(gh - 1)], gw_2[...])
     w_out = [send(gw_f.at[x], gw_f.at[x], dev_x(k)) for k in range(1, gx)]
 
+    last = len(started) - (gl * gh - 1) - len(w_out) - len(k_end)
+    for copy in started[:last]:
+        copy.wait_send()
     back_x = []
     for j in reversed(far_first):
         for m in range(gl):
@@ -357,7 +360,7 @@
         gw_ref[b * tx:(b + 1) * tx, :] = gw_f[b, :tx, :ih]
     for copy in back_x + k_end:
         copy.wait_recv()
-    for copy in started:
+    for copy in started[last:]:
         copy.wait_send()
 
 

time: 72.9 us -> 72.1 us (0.989)
  Pallas kernels: 72.1 us -> 71.3 us
    pallas_call x1, Pallas kernels: 71.1 us -> 70.3 us  [shards(): pl.pallas_call(functools.partial(kernel, dims), out_shape=(jax.ShapeDtype...]
where the time goes in v5:
time: 72.1 us; the launch traced here: 72 us
  Pallas kernels  71.3 us (99%)
    pallas_call x1, Pallas kernels, shards(): pl.pallas_call(functools.partial(kernel, dims), out_shape=(jax.ShapeDtype...  70.3 us

profile of v5, /device:TPU:1, one launch (start us, length us, event | category | flops | bytes accessed | tf_op | source)
XLA Modules:
  0.0 72.0 jit_solution(17741609626302549441)
XLA Ops:
  0.6 70.3 %shard_map.85 = (f32[1024,128]{1,0:T(8,128)S(1)}, f32[16,64]{1,0:T(8,128)S(1)}, f32[1024,128]{1,0:T(8,128)S(1)}) custom-call(bf16[16,576,128]{2,1,0:T(8,128)(2,1)} %bitcast.5, bf16[576,1024]{1,0:T(8,128)(2,1)} %bitcast.6, bf16[1024,128]{1,0:T(8,128)(2,1)} %bitcast.7, bf16[16,64]{1,0:T(8,128)(2,1)} %iw_in.1, bf16[1024,128]{1,0:T(8,128)(2,1)} %ik_in.1, ...), custom_call_target="tpu_custom_call" | custom-call | tf_op jit(solution)/shard_map/pallas_call | solution.py:390
  70.9 1.0 %shard_map.86 = (f32[1024,128]{1,0:T(8,128)}, f32[16,64]{1,0:T(8,128)}, f32[1024,128]{1,0:T(8,128)}) custom-call(f32[1024,128]{1,0:T(8,128)S(1)} %get-tuple-element.9.gq_ref, f32[16,64]{1,0:T(8,128)S(1)} %get-tuple-element.10.gw_ref, f32[1024,128]{1,0:T(8,128)S(1)} %get-tuple-element.11.kg_ref), custom_call_target="tpu_custom_call" | custom-call | tf_op jit(solution)/shard_map/pallas_call | solution.py:442
